TPU v7x, 256 devices: a whole 4x4x8 slice. The times are simulated.
256 devices in a mesh: row: 8 (over z_lo, y), col: 32 (over z_hi, x, core).
Axes of the slice: x: 4, y: 4, z: 8 (z_hi: 4, z_lo: 2; z = z_hi * 2 + z_lo), core: 2. Of those that a mesh axis runs over, the one named last changes fastest.
Arguments:
- activations: bfloat16 [1024, 8192], P('col', 'row'), may hold values from -6 to 6
- cotangent: bfloat16 [1024, 8192], P('col', 'row'), may hold values from -0.59765625 to 0.59765625
- gate_weight: bfloat16 [8192, 21504], P('row', 'col'), may hold values from -0.0625 to 0.0625
- up_weight: bfloat16 [8192, 21504], P('row', 'col'), may hold values from -0.0625 to 0.0625
- down_weight: bfloat16 [21504, 8192], P('col', 'row'), may hold values from -0.0390625 to 0.0390625
Outputs:
- input_grad: bfloat16 [1024, 8192], P('col', 'row')
- gate_grad: bfloat16 [8192, 21504], P('row', 'col')
- up_grad: bfloat16 [8192, 21504], P('row', 'col')
- down_grad: bfloat16 [21504, 8192], P('col', 'row')
All inputs are finite; a program needn't handle non-finite values.
Results may differ from a plain program's by a relative error of at most 0.005.
Values may be sent and summed in bfloat16 or wider, within the bound.
No kernel may reach another device: no remote copies, remote signals or barrier semaphores. Data moves between devices by JAX's collectives and lax.ppermute only.
A program may use at most 128 MiB of HBM per device.

v0:
```python
import jax
import jax.numpy as jnp
from jax import lax
from jax.sharding import PartitionSpec as P


def local_deltas(sums, hid_cols):
    gate = sums[:, :hid_cols]
    up = sums[:, hid_cols : 2 * hid_cols]
    hidden_grad = sums[:, 2 * hid_cols :]
    sigmoid_gate = jax.nn.sigmoid(gate)
    hidden = (gate * sigmoid_gate * up).astype(jnp.bfloat16)
    gate_delta = (hidden_grad * up * sigmoid_gate * (1.0 + gate * (1.0 - sigmoid_gate))).astype(
        jnp.bfloat16
    )
    up_delta = (hidden_grad * gate * sigmoid_gate).astype(jnp.bfloat16)
    return (hidden, gate_delta, up_delta)


def per_device(activations, cotangent, gate_weight, up_weight, down_weight):
    act_all, cot_all = (
        lax.all_gather(activations, "col", axis=0, tiled=True),
        lax.all_gather(cotangent, "col", axis=0, tiled=True),
    )
    hid_cols = gate_weight.shape[1]
    both_weights = jnp.concatenate([gate_weight, up_weight], axis=1)
    contract_cols = (((1,), (1,)), ((), ()))
    contract_rows = (((0,), (0,)), ((), ()))
    forward_part = jnp.dot(act_all, both_weights, preferred_element_type=jnp.float32)
    backward_part = lax.dot_general(
        cot_all, down_weight, contract_cols, preferred_element_type=jnp.float32
    )
    sums = lax.psum_scatter(
        jnp.concatenate([forward_part, backward_part], axis=1),
        "row",
        scatter_dimension=0,
        tiled=True,
    )
    hidden, gate_delta, up_delta = local_deltas(sums, hid_cols)
    hidden, gate_delta, up_delta = (
        lax.all_gather(hidden, "row", axis=0, tiled=True),
        lax.all_gather(gate_delta, "row", axis=0, tiled=True),
        lax.all_gather(up_delta, "row", axis=0, tiled=True),
    )
    down_grad = lax.dot_general(
        hidden, cot_all, contract_rows, preferred_element_type=jnp.float32
    ).astype(jnp.bfloat16)
    gate_grad = lax.dot_general(
        act_all, gate_delta, contract_rows, preferred_element_type=jnp.float32
    ).astype(jnp.bfloat16)
    up_grad = lax.dot_general(
        act_all, up_delta, contract_rows, preferred_element_type=jnp.float32
    ).astype(jnp.bfloat16)
    both_deltas = jnp.concatenate([gate_delta, up_delta], axis=1)
    input_grad = lax.psum_scatter(
        lax.dot_general(
            both_deltas, both_weights, contract_cols, preferred_element_type=jnp.float32
        ),
        "col",
        scatter_dimension=0,
        tiled=True,
    )
    return (input_grad.astype(jnp.bfloat16), gate_grad, up_grad, down_grad)


def solution(mesh):
    return jax.shard_map(
        per_device,
        mesh=mesh,
        in_specs=(
            P("col", "row"),
            P("col", "row"),
            P("row", "col"),
            P("row", "col"),
            P("col", "row"),
        ),
        out_specs=(P("col", "row"), P("row", "col"), P("row", "col"), P("col", "row")),
        check_vma=False,
    )
```

profile of v0, /device:TPU:8, one launch (start us, length us, event | category | flops | bytes accessed | tf_op | source)
XLA Modules:
  0.0 472.7 jit_solution(8116359554584954687)
XLA Ops:
  7.2 0.0 copy-start
  7.2 0.0 copy-start.2
  7.2 0.0 all-gather.8.cloned.1.call-start
  7.2 0.7 all-gather.8.cloned.1.call-update
  7.9 0.0 all-gather.6.cloned.1.call-start
  8.0 0.7 all-gather.6.cloned.1.call-update
  8.7 0.0 reduce-scatter.3.cloned.1.call-start
  8.7 2.6 constant_dynamic-update-slice_fusion.1
  11.3 0.0 copy-done.2
  11.3 1.2 constant_dynamic-update-slice_fusion
  12.5 55.7 %all-gather.8.cloned.1.call-done = bf16[1024,1024]{1,0:T(8,128)(2,1)} async-done(((bf16[32,1024]{1,0:T(8,128)(2,1)}), bf16[1024,1024]{1,0:T(8,128)(2,1)}) %all-gather.8.cloned.1.call-update) | async-done | bytes 2097168 | tf_op jit(solution)/shard_map/all_gather | solution.py:23
  68.2 0.0 copy-done
  68.2 4.8 %fusion.7 = f32[1024,672]{0,1:T(8,128)} fusion(bf16[1024,1024]{1,0:T(8,128)(2,1)} %all-gather.8.cloned.1.call-done, bf16[672,1024]{1,0:T(8,128)(2,1)S(1)} %copy-done), kind=kOutput, calls=%fused_computation.18 | convolution fusion | flops 1409286144 | bytes 6225920 | tf_op jit(solution)/shard_map/dot_general | solution.py:30
  73.0 49.5 %all-gather.6.cloned.1.call-done = bf16[1024,1024]{1,0:T(8,128)(2,1)} async-done(((bf16[32,1024]{1,0:T(8,128)(2,1)}), bf16[1024,1024]{1,0:T(8,128)(2,1)}) %all-gather.6.cloned.1.call-update) | async-done | bytes 2097168 | tf_op jit(solution)/shard_map/all_gather | solution.py:22
  122.4 0.0 copy-start.1
  122.4 5.6 %convolution_bitcast_fusion = f32[1024,1344]{0,1:T(8,128)S(1)} fusion(bf16[1024,1344]{0,1:T(8,128)(2,1)} %constant_dynamic-update-slice_fusion, bf16[1024,1024]{1,0:T(8,128)(2,1)} %all-gather.6.cloned.1.call-done), kind=kOutput, calls=%fused_computation.1 | convolution fusion | flops 2818572288 | bytes 10354688 | tf_op jit(solution)/shard_map/dot_general | solution.py:29
  128.1 0.0 copy-done.1
  128.1 4.9 %pad_maximum_fusion = f32[1024,2016]{0,1:T(8,128)} fusion(f32[1024,672]{0,1:T(8,128)S(1)} %copy-done.1, f32[1024,1344]{0,1:T(8,128)S(1)} %convolution_bitcast_fusion), kind=kLoop, calls=%fused_computation | loop fusion | flops 2064384 | bytes 16515072 | tf_op jit(solution)/shard_map/concatenate | solution.py:34
  133.0 0.0 reduce-scatter.3.cloned.1.call-update
  133.0 0.0 all-gather.10.cloned.1.call-start
  133.1 89.0 %reduce-scatter.3.cloned.1.call-done = f32[128,2016]{0,1:T(8,128)} async-done(((f32[1024,2016]{0,1:T(8,128)}), f32[128,2016]{0,1:T(8,128)}) %reduce-scatter.3.cloned.1.call-update) | async-done | bytes 1032208 | tf_op jit(solution)/shard_map/reduce_scatter | solution.py:33
  222.0 2.1 multiply_convert_fusion
  224.1 0.0 all-gather.10.cloned.1.call-update
  224.2 0.0 all-gather.12.cloned.1.call-start
  224.2 0.5 all-gather.12.cloned.1.call-update
  224.8 0.0 all-gather.14.cloned.1.call-start
  224.8 0.5 all-gather.14.cloned.1.call-update
  225.3 0.2 reduce-scatter.5.cloned.1.call-start
  225.6 41.6 %all-gather.10.cloned.1.call-done = bf16[1024,672]{0,1:T(8,128)(2,1)} async-done(((bf16[128,672]{0,1:T(8,128)(2,1)}), bf16[1024,672]{0,1:T(8,128)(2,1)}) %all-gather.10.cloned.1.call-update) | async-done | bytes 1376272 | tf_op jit(solution)/shard_map/all_gather | solution.py:42
  267.2 45.7 %all-gather.12.cloned.1.call-done = bf16[1024,672]{0,1:T(8,128)(2,1)} async-done(((bf16[128,672]{0,1:T(8,128)(2,1)}), bf16[1024,672]{0,1:T(8,128)(2,1)}) %all-gather.12.cloned.1.call-update) | async-done | bytes 1376272 | tf_op jit(solution)/shard_map/all_gather | solution.py:43
  312.9 8.2 %fusion = f32[1024,1024]{1,0:T(8,128)} fusion(bf16[1024,1344]{0,1:T(8,128)(2,1)} %constant_dynamic-update-slice_fusion, bf16[1024,672]{0,1:T(8,128)(2,1)} %all-gather.12.cloned.1.call-done, bf16[1024,672]{0,1:T(8,128)(2,1)} %all-gather.10.cloned.1.call-done), kind=kOutput, calls=%fused_computation.2 | convolution fusion | flops 2824077312 | bytes 9699328 | tf_op jit(solution)/shard_map/dot_general | solution.py:56
  321.0 0.0 copy-start.4
  321.0 0.0 reduce-scatter.5.cloned.1.call-update
  321.1 1.6 copy-done.4
  322.6 0.0 copy-start.5
  322.6 0.0 copy-start.6
  322.6 4.2 fusion.5
  326.8 0.0 copy-done.5
  326.8 0.0 copy-done.6
  326.8 0.0 copy-start.3
  326.8 2.7 fusion.4
  329.5 29.1 %all-gather.14.cloned.1.call-done = bf16[1024,672]{0,1:T(8,128)(2,1)} async-done(((bf16[128,672]{0,1:T(8,128)(2,1)}), bf16[1024,672]{0,1:T(8,128)(2,1)}) %all-gather.14.cloned.1.call-update) | async-done | bytes 1376272 | tf_op jit(solution)/shard_map/all_gather | solution.py:41
  358.5 0.0 copy-done.3
  358.6 4.0 convolution_convert_fusion
  362.6 101.8 %reduce-scatter.5.cloned.1.call-done = f32[32,1024]{1,0:T(8,128)} async-done(((f32[1024,1024]{1,0:T(8,128)}), f32[32,1024]{1,0:T(8,128)}) %reduce-scatter.5.cloned.1.call-update) | async-done | bytes 131088 | tf_op jit(solution)/shard_map/reduce_scatter | solution.py:55
  464.4 1.5 convert_element_type.29
Async XLA Ops:
  7.2 61.0 %copy-start = (bf16[672,1024]{1,0:T(8,128)(2,1)S(1)}, bf16[672,1024]{1,0:T(8,128)(2,1)}, u32[]{:S(2)}) copy-start(bf16[672,1024]{1,0:T(8,128)(2,1)} %param.9) | copy-start | bytes 4128772
  7.2 4.1 copy-start.2
  7.2 61.0 %all-gather.8.cloned.1.call-start = ((), (), s32[]{:S(2)}) async-start(), calls=%async_computation.3 | async-start | bytes 2162688 | tf_op jit(solution)/shard_map/all_gather | solution.py:23
  7.9 114.5 %all-gather.6.cloned.1.call-start = ((), (), s32[]{:S(2)}) async-start(), calls=%async_computation.2 | async-start | bytes 2162688 | tf_op jit(solution)/shard_map/all_gather | solution.py:22
  8.7 213.3 %reduce-scatter.3.cloned.1.call-start = ((), (), s32[]{:S(2)}) async-start(), calls=%async_computation.4 | async-start | bytes 9289728 | tf_op jit(solution)/shard_map/reduce_scatter | solution.py:33
  122.4 5.6 %copy-start.1 = (f32[1024,672]{0,1:T(8,128)S(1)}, f32[1024,672]{0,1:T(8,128)}, u32[]{:S(2)}) copy-start(f32[1024,672]{0,1:T(8,128)} %fusion.7) | copy-start | bytes 8257540
  133.0 134.2 %all-gather.10.cloned.1.call-start = ((), (), s32[]{:S(2)}) async-start(), calls=%async_computation.5 | async-start | bytes 1548288 | tf_op jit(solution)/shard_map/all_gather | solution.py:42
  224.2 88.7 %all-gather.12.cloned.1.call-start = ((), (), s32[]{:S(2)}) async-start(), calls=%async_computation.6 | async-start | bytes 1548288 | tf_op jit(solution)/shard_map/all_gather | solution.py:43
  224.8 133.8 %all-gather.14.cloned.1.call-start = ((), (), s32[]{:S(2)}) async-start(), calls=%async_computation.8 | async-start | bytes 1548288 | tf_op jit(solution)/shard_map/all_gather | solution.py:41
  225.3 239.0 %reduce-scatter.5.cloned.1.call-start = ((), (), s32[]{:S(2)}) async-start(), calls=%async_computation.7 | async-start | bytes 4325376 | tf_op jit(solution)/shard_map/reduce_scatter | solution.py:55
  321.0 1.6 copy-start.4
  322.6 4.2 copy-start.5
  322.6 4.2 copy-start.6
  326.8 31.8 %copy-start.3 = (bf16[1024,1024]{1,0:T(8,128)(2,1)S(1)}, bf16[1024,1024]{1,0:T(8,128)(2,1)}, u32[]{:S(2)}) copy-start(bf16[1024,1024]{1,0:T(8,128)(2,1)} %all-gather.8.cloned.1.call-done) | copy-start | bytes 6291460
Sparse Core Ops, SparseCore 0:
  10.6 57.5 all-gather.7
  70.7 51.6 all-gather.5
  133.1 88.8 reduce-scatter.2
  224.3 42.8 all-gather.9
  269.4 43.3 all-gather.11
  315.1 43.3 all-gather.13
  363.0 101.3 reduce-scatter.4
where the time goes:
time: 473 us
  waiting for transfers between devices  415 us (88%)
  matrix products  29.4 us (6%)
  between operations  14.2 us (3%)
  other arithmetic  8.58 us (2%)
  local copies, waits for them, and re-layouts  5.38 us (1%)
    reduce_scatter x1, waiting for transfers between devices, per_device(): lax.psum_scatter(lax.dot_general(both_deltas, both_weights, contract_cols...  102 us
    reduce_scatter x1, waiting for transfers between devices, per_device(): lax.psum_scatter(jnp.concatenate([forward_part, backward_part], axis=1),...  89 us
    all_gather x1, waiting for transfers between devices, per_device(): lax.all_gather(cotangent, 'col', axis=0, tiled=True)  55.7 us
    all_gather x1, waiting for transfers between devices, per_device(): lax.all_gather(activations, 'col', axis=0, tiled=True)  49.5 us
    all_gather x1, waiting for transfers between devices, per_device(): lax.all_gather(up_delta, 'row', axis=0, tiled=True)  45.7 us
    all_gather x1, waiting for transfers between devices, per_device(): lax.all_gather(gate_delta, 'row', axis=0, tiled=True)  41.6 us
    all_gather x1, waiting for transfers between devices, per_device(): lax.all_gather(hidden, 'row', axis=0, tiled=True)  29.1 us
  transfers between devices with their start and end apart: 7, of which 7 were waited for; matrix products, arithmetic and copies ran while one was open for 6% of the time, Pallas kernels for 0%

commit v1 on v0

v1 whole, which is shorter than its diff:
```python
import functools

import jax
import jax.numpy as jnp
from jax import lax
from jax.experimental import pallas as pl
from jax.experimental.pallas import tpu as pltpu
from jax.sharding import PartitionSpec as P

BF16, F32 = jnp.bfloat16, jnp.float32
NY, NZH, NX = 4, 4, 4
CHUNKS = ((0, 1), (2, 3))
RS_RING = False
AG_RING = False
C_DTYPE = BF16
ZH_DTYPE = BF16

NT = (((1,), (1,)), ((), ()))
NN = (((1,), (0,)), ((), ()))
TN = (((0,), (0,)), ((), ()))


def dot(a, b, dims):
    return lax.dot_general(a, b, dims, preferred_element_type=F32)


def shift_y(v, k):
    return lax.ppermute(v, "row", [(z * NY + y, z * NY + (y + k) % NY) for z in range(2) for y in range(NY)])


def swap_zl(v):
    return lax.ppermute(v, "row", [(r, (r + NY) % (2 * NY)) for r in range(2 * NY)])


def shift_col(v, dzh=0, dx=0, dc=0):
    pairs = []
    for zh in range(NZH):
        for x in range(NX):
            for c in range(2):
                at = (zh * NX + x) * 2 + c
                to = (((zh + dzh) % NZH) * NX + (x + dx) % NX) * 2 + (c + dc) % 2
                pairs.append((at, to))
    return lax.ppermute(v, "col", pairs)


def cost(flops, bytes_accessed):
    return pl.CostEstimate(flops=int(flops), bytes_accessed=int(bytes_accessed), transcendentals=0)


def nbytes(*arrays):
    return sum(a.size * a.dtype.itemsize for a in arrays)


def call(kernel, y, inputs, specs, outs, flops, name):
    return pl.pallas_call(
        kernel,
        out_shape=outs,
        grid_spec=pltpu.PrefetchScalarGridSpec(
            num_scalar_prefetch=1,
            grid=(1,),
            in_specs=specs,
            out_specs=[whole(o) for o in outs],
        ),
        compiler_params=pltpu.CompilerParams(vmem_limit_bytes=56 * 2**20),
        cost_estimate=cost(flops, nbytes(*inputs, *outs)),
        name=name,
    )(y, *inputs)


def whole(a):
    return pl.BlockSpec(a.shape, lambda i, y, n=len(a.shape): (0,) * n)


def weight_block(w, k):
    return pl.BlockSpec((1,) + w.shape[1:], lambda i, y: ((y[0] + k) % NY, 0, 0))


def partial_kernel(ks, adds, n_adds, y_ref, *refs):
    halves, refs = refs[:2], refs[2:]
    weights, refs = refs[: 3 * len(ks)], refs[3 * len(ks) :]
    added, outs = refs[:n_adds], refs[n_adds:]
    for i in range(len(ks)):
        for h in range(2):
            for m in range(3):
                part = dot(weights[3 * i + m][0], halves[h][1 if m == 2 else 0], NT)
                for at, half in adds[i]:
                    if half is None:
                        part = part + added[at][h, m].astype(F32)
                    elif half == h:
                        part = part + added[at][m].astype(F32)
                outs[i][h, m] = part.astype(outs[i].dtype)


def partials(y, halves, weights, ks, adds, added, dtype, name):
    rows, tokens = weights[0].shape[1], halves[0].shape[1]
    outs = [jax.ShapeDtypeStruct((2, 3, rows, tokens), dtype) for _ in ks]
    specs = [whole(h) for h in halves]
    inputs = list(halves)
    for k in ks:
        for w in weights:
            inputs.append(w)
            specs.append(weight_block(w, k))
    for a in added:
        inputs.append(a)
        specs.append(whole(a))
    flops = 2 * len(ks) * 6 * rows * tokens * weights[0].shape[2]
    return call(functools.partial(partial_kernel, ks, adds, len(added)), y, inputs, specs, outs, flops, name)


def deltas(sums):
    gate, up, hidden_grad = sums[:, 0], sums[:, 1], sums[:, 2]
    s = jax.nn.sigmoid(gate)
    hidden = (gate * s * up).astype(BF16)
    gate_delta = (hidden_grad * up * s * (1.0 + gate * (1.0 - s))).astype(BF16)
    up_delta = (hidden_grad * gate * s).astype(BF16)
    return jnp.stack([hidden, gate_delta, up_delta], axis=1)


def delta_at(group, k, h, m):
    if k == 2 and len(group) == 5:
        return group[2 + h][m]
    return group[k if k < 3 else len(group) - 1][h, m]


def input_kernel(n, y_ref, gate_ref, up_ref, *refs):
    group, (own, other) = refs[:n], refs[n:]
    for h, out in ((0, own), (1, other)):
        total = None
        for k in range(NY):
            block = lax.rem(y_ref[0] + NY - k, NY)
            for m, w in ((1, gate_ref), (2, up_ref)):
                term = dot(delta_at(group, k, h, m), w[block], TN)
                total = term if total is None else total + term
        out[...] = total.astype(out.dtype)


def input_part(y, gate_w, up_w, group):
    tokens, feats = group[0].shape[-1], gate_w.shape[2]
    outs = [jax.ShapeDtypeStruct((tokens, feats), F32), jax.ShapeDtypeStruct((tokens, feats), C_DTYPE)]
    inputs = [gate_w, up_w, *group]
    flops = 2 * 2 * tokens * 2 * NY * gate_w.shape[1] * feats
    return call(functools.partial(input_kernel, len(group)), y, inputs, [whole(a) for a in inputs], outs, flops, "input_part")


def grads_kernel(layout, y_ref, *refs):
    n = sum(2 + g for g in layout)
    ins, (down, gate, up) = refs[:n], refs[n:]
    chunks, at = [], 0
    for g in layout:
        chunks.append((ins[at : at + 2], ins[at + 2 : at + 2 + g]))
        at += 2 + g
    for k in range(NY):
        block = lax.rem(y_ref[0] + NY - k, NY)
        for m, out in ((0, down), (1, gate), (2, up)):
            total = None
            for halves, group in chunks:
                for h in range(2):
                    term = dot(delta_at(group, k, h, m), halves[h][1 if m == 0 else 0], NN)
                    total = term if total is None else total + term
            out[block] = total.astype(out.dtype)


def weight_grads(y, chunks, shape):
    inputs, layout = [], []
    for halves, group in chunks:
        inputs += [*halves, *group]
        layout.append(len(group))
    outs = [jax.ShapeDtypeStruct(shape, BF16)] * 3
    tokens = sum(2 * h[0].shape[1] for h, _ in chunks)
    flops = 2 * 3 * tokens * shape[0] * shape[1] * shape[2]
    return call(functools.partial(grads_kernel, layout), y, inputs, [whole(a) for a in inputs], outs, flops, "weight_grads")


def per_device(activations, cotangent, gate_weight, up_weight, down_weight):
    y = lax.rem(lax.axis_index("row"), NY)[None].astype(jnp.int32)
    rows, feats = activations.shape
    hid = gate_weight.shape[1]
    shape = (NY, hid // NY, feats)
    weights = [w.reshape(shape) for w in (gate_weight.T, up_weight.T, down_weight)]

    both = jnp.stack([activations, cotangent])
    mine = jnp.stack([both] + [shift_col(both, dzh=k) for k in range(1, NZH)], axis=1)
    mine = mine.reshape(2, NZH * rows, feats)
    moved = {s: shift_col(mine, dx=s) if s else mine for s in sum(CHUNKS, ())}

    done, input_sums = [], None
    for chunk in CHUNKS:
        own = jnp.concatenate([moved[s] for s in chunk], axis=1) if len(chunk) > 1 else moved[chunk[0]]
        halves = (own, shift_col(own, dc=1))
        if RS_RING:
            (far,) = partials(y, halves, weights, (2,), ((),), (), BF16, "partial_far")
            a, b = shift_y(far[0], 1), shift_y(far[1], -1)
            right, left = partials(y, halves, weights, (1, 3), (((0, 0),), ((1, 1),)), (a, b), BF16, "partial_near")
            arrived = [shift_y(right, 1), shift_y(left, -1)]
        else:
            out = partials(y, halves, weights, (2, 1, 3), ((), (), ()), (), BF16, "partial_sent")
            arrived = [shift_y(v, k) for v, k in zip(out, (2, 1, -1))]
        (sums,) = partials(y, halves, weights, (0,), (tuple((i, None) for i in range(len(arrived))),), arrived, F32, "partial_own")
        d0 = deltas(sums + swap_zl(sums))
        d1, d3 = shift_y(d0, 1), shift_y(d0, -1)
        if AG_RING:
            group = (d0, d1, shift_y(d1[0], 1), shift_y(d3[1], -1), d3)
        else:
            group = (d0, d1, shift_y(d0, 2), d3)
        done.append((halves, group))

        keep, send = input_part(y, weights[0], weights[1], group)
        pair = keep + shift_col(send, dc=1).astype(F32)
        pair = pair.reshape(len(chunk), NZH * rows, feats)
        for i, s in enumerate(chunk):
            part = shift_col(pair[i].astype(BF16), dx=-s).astype(F32) if s else pair[i]
            input_sums = part if input_sums is None else input_sums + part

    input_sums = input_sums.reshape(NZH, rows, feats)
    input_grad = input_sums[0]
    for k in range(1, NZH):
        input_grad = input_grad + shift_col(input_sums[k].astype(ZH_DTYPE), dzh=-k).astype(F32)
    down_grad, gate_grad, up_grad = weight_grads(y, done, shape)
    return (
        input_grad.astype(BF16),
        gate_grad.reshape(hid, feats).T,
        up_grad.reshape(hid, feats).T,
        down_grad.reshape(hid, feats),
    )


def solution(mesh):
    return jax.shard_map(
        per_device,
        mesh=mesh,
        in_specs=(P("col", "row"), P("col", "row"), P("row", "col"), P("row", "col"), P("col", "row")),
        out_specs=(P("col", "row"), P("row", "col"), P("row", "col"), P("col", "row")),
        check_vma=False,
    )
```

time: 473 us -> 207 us (0.44)
  waiting for transfers between devices: 415 us -> 102 us
  starting transfers between devices: 0.45 us -> 47.9 us
  Pallas kernels: 0 us -> 42.2 us
  matrix products: 29.4 us -> 0 us
  between operations: 14.2 us -> 0.91 us
  other arithmetic: 8.58 us -> 2.92 us
    all_gather x5 -> x0, waiting for transfers between devices: 222 us -> none  [the longest x1 55.7 us: per_device(): lax.all_gather(cotangent, 'col', axis=0, tiled=True)]
    reduce_scatter x2 -> x0, waiting for transfers between devices: 191 us -> none  [the longest x1 102 us: per_device(): lax.psum_scatter(lax.dot_general(both_deltas, both_weights, contract_cols...]
    ppermute x0 -> x30, waiting for transfers between devices: none -> 102 us  [the longest x16 42.2 us: shift_col(): return lax.ppermute(v, 'col', pairs)]
    ppermute x0 -> x30, starting transfers between devices: none -> 47.9 us  [the longest x16 28.9 us: shift_col(): return lax.ppermute(v, 'col', pairs)]
    pallas_call x0 -> x7, Pallas kernels: none -> 42.2 us  [call(): pl.pallas_call(kernel, out_shape=outs, grid_spec=pltpu.PrefetchScalarGrid...]
    dot_general x6 -> x0, matrix products: 29.4 us -> none  [the longest x1 8.17 us: per_device(): lax.dot_general(both_deltas, both_weights, contract_cols, preferred_eleme...]
    concatenate x1, other arithmetic: 4.91 us -> 0.07 us  [per_device(): jnp.concatenate([moved[s] for s in chunk], axis=1)]
  transfers between devices with their start and end apart: 7 -> 30, of which waited for: 7 -> 17; matrix products, arithmetic and copies ran while one was open for 6% -> 1% of each run, Pallas kernels for 0% -> 21%
where the time goes in v1:
time: 207 us; the launch traced here: 203 us
  waiting for transfers between devices  102 us (49%)
  starting transfers between devices  47.9 us (23%)
  Pallas kernels  42.2 us (20%)
  local copies, waits for them, and re-layouts  6.85 us (3%)
  other arithmetic  2.92 us (1%)
    ppermute x16, waiting for transfers between devices, shift_col(): return lax.ppermute(v, 'col', pairs)  42.2 us
    pallas_call x7, Pallas kernels, call(): pl.pallas_call(kernel, out_shape=outs, grid_spec=pltpu.PrefetchScalarGrid...  42.2 us
    ppermute x12, waiting for transfers between devices, shift_y(): lax.ppermute(v, 'row', [(z * NY + y, z * NY + (y + k) % NY) for z in rang...  41.1 us
    ppermute x16, starting transfers between devices, shift_col(): return lax.ppermute(v, 'col', pairs)  28.9 us
    ppermute x12, starting transfers between devices, shift_y(): lax.ppermute(v, 'row', [(z * NY + y, z * NY + (y + k) % NY) for z in rang...  19.1 us
    ppermute x2, waiting for transfers between devices, swap_zl(): lax.ppermute(v, 'row', [(r, (r + NY) % (2 * NY)) for r in range(2 * NY)])  18.9 us
    unnamed x43, local copies, waits for them, and re-layouts  6.7 us
  transfers between devices with their start and end apart: 30, of which 17 were waited for; matrix products, arithmetic and copies ran while one was open for 1% of the time, Pallas kernels for 21%

profile of v1, /device:TPU:8, one launch (start us, length us, event | category | flops | bytes accessed | tf_op | source)
XLA Modules:
  0.0 203.0 jit_solution(16644511825264256332)
XLA Ops:
  0.6 0.9 fusion.5
  1.5 7.3 %collective-permute-start.1 = (bf16[2,32,1024]{2,1,0:T(8,128)(2,1)S(1)}, bf16[2,32,1024]{2,1,0:T(8,128)(2,1)S(1)}, u32[]{:S(2)}, u32[]{:S(2)}) collective-permute-start(bf16[2,32,1024]{2,1,0:T(8,128)(2,1)S(1)} %get-tuple-element.44), channel_id=1, source_target_pairs={{0,16},{1,17},{2,18},{3,19},{4,20},{5,21},{6,22},{7,23},{8,24},{9,... | collective-permute-start | bytes 393224 | tf_op jit(solution)/shard_map/ppermute | solution.py:43
  8.8 1.5 collective-permute-start
  10.3 2.7 %collective-permute-start.2 = (bf16[2,32,1024]{2,1,0:T(8,128)(2,1)S(1)}, bf16[2,32,1024]{2,1,0:T(8,128)(2,1)S(1)}, u32[]{:S(2)}, u32[]{:S(2)}) collective-permute-start(bf16[2,32,1024]{2,1,0:T(8,128)(2,1)S(1)} %get-tuple-element.44), channel_id=1, source_target_pairs={{0,24},{1,25},{2,26},{3,27},{4,28},{5,29},{6,30},{7,31},{8,0},{9,1... | collective-permute-start | bytes 393224 | tf_op jit(solution)/shard_map/ppermute | solution.py:43
  12.9 2.3 %collective-permute-done.1 = bf16[2,32,1024]{2,1,0:T(8,128)(2,1)S(1)} collective-permute-done((bf16[2,32,1024]{2,1,0:T(8,128)(2,1)S(1)}, bf16[2,32,1024]{2,1,0:T(8,128)(2,1)S(1)}, u32[]{:S(2)}, u32[]{:S(2)}) %collective-permute-start.1) | collective-permute-done | bytes 131104 | tf_op jit(solution)/shard_map/ppermute | solution.py:43
  15.2 4.2 %collective-permute-done = bf16[2,32,1024]{2,1,0:T(8,128)(2,1)S(1)} collective-permute-done((bf16[2,32,1024]{2,1,0:T(8,128)(2,1)S(1)}, bf16[2,32,1024]{2,1,0:T(8,128)(2,1)S(1)}, u32[]{:S(2)}, u32[]{:S(2)}) %collective-permute-start) | collective-permute-done | bytes 131104 | tf_op jit(solution)/shard_map/ppermute | solution.py:43
  19.4 1.9 collective-permute-done.2
  21.4 3.1 %collective-permute-start.14 = (bf16[2,128,1024]{2,1,0:T(8,128)(2,1)S(1)}, bf16[2,128,1024]{2,1,0:T(8,128)(2,1)S(1)}, u32[]{:S(2)}, u32[]{:S(2)}) collective-permute-start(bf16[2,128,1024]{2,1,0:T(8,128)(2,1)S(1)} %bitcast.51), channel_id=1, source_target_pairs={{0,4},{1,5},{2,6},{3,7},{4,0},{5,1},{6,2},{7,3},{8,12},{9,13},{10,... | collective-permute-start | bytes 1572872 | tf_op jit(solution)/shard_map/ppermute | solution.py:43
  24.6 1.1 collective-permute-start.15
  25.7 0.9 collective-permute-start.3
  26.6 11.3 %collective-permute-done.14 = bf16[2,128,1024]{2,1,0:T(8,128)(2,1)S(1)} collective-permute-done((bf16[2,128,1024]{2,1,0:T(8,128)(2,1)S(1)}, bf16[2,128,1024]{2,1,0:T(8,128)(2,1)S(1)}, u32[]{:S(2)}, u32[]{:S(2)}) %collective-permute-start.14) | collective-permute-done | bytes 524320 | tf_op jit(solution)/shard_map/ppermute | solution.py:43
  37.9 10.3 %collective-permute-done.15 = bf16[2,128,1024]{2,1,0:T(8,128)(2,1)S(1)} collective-permute-done((bf16[2,128,1024]{2,1,0:T(8,128)(2,1)S(1)}, bf16[2,128,1024]{2,1,0:T(8,128)(2,1)S(1)}, u32[]{:S(2)}, u32[]{:S(2)}) %collective-permute-start.15) | collective-permute-done | bytes 524320 | tf_op jit(solution)/shard_map/ppermute | solution.py:43
  49.0 2.0 collective-permute-done.16.refs_1_.refs_7_
  51.0 1.0 copy-done.2
  52.0 6.4 %partial_sent.3 = (bf16[2,3,168,256]{3,2,1,0:T(8,128)(2,1)}, bf16[2,3,168,256]{3,2,1,0:T(8,128)(2,1)}, bf16[2,3,168,256]{3,2,1,0:T(8,128)(2,1)}) custom-call(s32[1]{0:T(128)} %bitcast.y_ref, bf16[2,256,1024]{2,1,0:T(8,128)(2,1)} %copy-done.1, bf16[2,256,1024]{2,1,0:T(8,128)(2,1)} %copy-done.2, bf16[4,168,1024]{2,1,0:T(8,128)(2,1)} %bitcast.31, ...), custom_call_target="tpu_custom_call" | custom-call | flops 1585446912 | bytes 16031744 | tf_op jit(solution)/shard_map/partial_sent/pallas_call | solution.py:55
  58.4 2.3 %collective-permute-start.17 = (bf16[2,3,168,256]{3,2,1,0:T(8,128)(2,1)}, bf16[2,3,168,256]{3,2,1,0:T(8,128)(2,1)S(1)}, u32[]{:S(2)}, u32[]{:S(2)}) collective-permute-start(bf16[2,3,168,256]{3,2,1,0:T(8,128)(2,1)} %get-tuple-element.22), channel_id=1, source_target_pairs={{0,64},{32,96},{64,0},{96,32},{128,192},{160,224},{192,128},{224,1... | collective-permute-start | bytes 1548296 | tf_op jit(solution)/shard_map/ppermute | solution.py:28
  60.7 2.0 collective-permute-start.19
  62.7 6.5 %partial_sent.2 = (bf16[2,3,168,256]{3,2,1,0:T(8,128)(2,1)}, bf16[2,3,168,256]{3,2,1,0:T(8,128)(2,1)}, bf16[2,3,168,256]{3,2,1,0:T(8,128)(2,1)}) custom-call(s32[1]{0:T(128)} %bitcast.y_ref, bf16[2,256,1024]{2,1,0:T(8,128)(2,1)} %copy-done, bf16[2,256,1024]{2,1,0:T(8,128)(2,1)} %collective-permute-done.4.refs_1_, bf16[4,168,1024]{2,1,0:T(8,128)(2,1)} %bitcast.34, ...), custom_call_target="tpu_custom_call" | custom-call | flops 1585446912 | bytes 16031744 | tf_op jit(solution)/shard_map/partial_sent/pallas_call | solution.py:55
  69.2 1.4 collective-permute-start.5
  70.6 2.6 %collective-permute-start.6 = (bf16[2,3,168,256]{3,2,1,0:T(8,128)(2,1)}, bf16[2,3,168,256]{3,2,1,0:T(8,128)(2,1)S(1)}, u32[]{:S(2)}, u32[]{:S(2)}) collective-permute-start(bf16[2,3,168,256]{3,2,1,0:T(8,128)(2,1)} %get-tuple-element.18), channel_id=1, source_target_pairs={{0,32},{32,64},{64,96},{96,0},{128,160},{160,192},{192,224},{224,1... | collective-permute-start | bytes 1548296 | tf_op jit(solution)/shard_map/ppermute | solution.py:28
  73.2 1.6 collective-permute-done.17.refs_5_
  75.2 10.7 %collective-permute-done.18.refs_6_ = bf16[2,3,168,256]{3,2,1,0:T(8,128)(2,1)S(1)} collective-permute-done((bf16[2,3,168,256]{3,2,1,0:T(8,128)(2,1)}, bf16[2,3,168,256]{3,2,1,0:T(8,128)(2,1)S(1)}, u32[]{:S(2)}, u32[]{:S(2)}) %collective-permute-start.18) | collective-permute-done | bytes 516128 | tf_op jit(solution)/shard_map/ppermute | solution.py:28
  87.5 4.5 %partial_own.3 = f32[2,3,168,256]{3,2,1,0:T(8,128)} custom-call(s32[1]{0:T(128)} %bitcast.y_ref, bf16[2,256,1024]{2,1,0:T(8,128)(2,1)} %copy-done.1, bf16[2,256,1024]{2,1,0:T(8,128)(2,1)} %copy-done.2, bf16[4,168,1024]{2,1,0:T(8,128)(2,1)} %bitcast.37, bf16[4,168,1024]{2,1,0:T(8,128)(2,1)} %bitcast.47, bf16[4,168,1024]{2,1,0:T(8,128)(2,1)} %bitcast.29, ...), custom_call_target="tpu_custom_call" | custom-call | flops 528482304 | bytes 8806400 | tf_op jit(solution)/shard_map/partial_own/pallas_call | solution.py:55
  92.0 4.9 %collective-permute-done.5.refs_5_ = bf16[2,3,168,256]{3,2,1,0:T(8,128)(2,1)S(1)} collective-permute-done((bf16[2,3,168,256]{3,2,1,0:T(8,128)(2,1)}, bf16[2,3,168,256]{3,2,1,0:T(8,128)(2,1)S(1)}, u32[]{:S(2)}, u32[]{:S(2)}) %collective-permute-start.5) | collective-permute-done | bytes 516128 | tf_op jit(solution)/shard_map/ppermute | solution.py:28
  96.9 10.4 %collective-permute-done.6.refs_6_ = bf16[2,3,168,256]{3,2,1,0:T(8,128)(2,1)S(1)} collective-permute-done((bf16[2,3,168,256]{3,2,1,0:T(8,128)(2,1)}, bf16[2,3,168,256]{3,2,1,0:T(8,128)(2,1)S(1)}, u32[]{:S(2)}, u32[]{:S(2)}) %collective-permute-start.6) | collective-permute-done | bytes 516128 | tf_op jit(solution)/shard_map/ppermute | solution.py:28
  108.9 4.5 %partial_own.2 = f32[2,3,168,256]{3,2,1,0:T(8,128)} custom-call(s32[1]{0:T(128)} %bitcast.y_ref, bf16[2,256,1024]{2,1,0:T(8,128)(2,1)} %copy-done, bf16[2,256,1024]{2,1,0:T(8,128)(2,1)} %collective-permute-done.4.refs_1_, bf16[4,168,1024]{2,1,0:T(8,128)(2,1)} %bitcast.38, bf16[4,168,1024]{2,1,0:T(8,128)(2,1)} %bitcast.48, bf16[4,168,1024]{2,1,0:T(8,128)(2,1)} %bitcast.30, ...), custom_call_target="tpu_custom_call" | custom-call | flops 528482304 | bytes 8806400 | tf_op jit(solution)/shard_map/partial_own/pallas_call | solution.py:55
  113.4 2.7 %collective-permute-done.20 = f32[2,3,168,256]{3,2,1,0:T(8,128)S(1)} collective-permute-done((f32[2,3,168,256]{3,2,1,0:T(8,128)}, f32[2,3,168,256]{3,2,1,0:T(8,128)S(1)}, u32[]{:S(2)}, u32[]{:S(2)}) %collective-permute-start.20) | collective-permute-done | bytes 1032224 | tf_op jit(solution)/shard_map/ppermute | solution.py:32
  116.6 1.6 collective-permute-start.23
  118.2 1.2 collective-permute-start.22
  119.3 2.5 %collective-permute-start.21 = (bf16[2,3,168,256]{3,2,1,0:T(8,128)(2,1)S(1)}, bf16[2,3,168,256]{3,2,1,0:T(8,128)(2,1)S(1)}, u32[]{:S(2)}, u32[]{:S(2)}) collective-permute-start(bf16[2,3,168,256]{3,2,1,0:T(8,128)(2,1)S(1)} %pad_maximum_fusion.3.refs_0_.refs_8_), channel_id=1, source_target_pairs={{0,32},{32,64},{64,96},{96,0},{128,160},{160,192},{192,224},{224,1... | collective-permute-start | bytes 1548296 | tf_op jit(solution)/shard_map/ppermute | solution.py:28
  121.9 16.1 %collective-permute-done.8 = f32[2,3,168,256]{3,2,1,0:T(8,128)S(1)} collective-permute-done((f32[2,3,168,256]{3,2,1,0:T(8,128)}, f32[2,3,168,256]{3,2,1,0:T(8,128)S(1)}, u32[]{:S(2)}, u32[]{:S(2)}) %collective-permute-start.8) | collective-permute-done | bytes 1032224 | tf_op jit(solution)/shard_map/ppermute | solution.py:32
  138.4 1.3 collective-permute-start.11
  139.7 1.2 collective-permute-start.10
  140.9 2.5 %collective-permute-start.9 = (bf16[2,3,168,256]{3,2,1,0:T(8,128)(2,1)S(1)}, bf16[2,3,168,256]{3,2,1,0:T(8,128)(2,1)S(1)}, u32[]{:S(2)}, u32[]{:S(2)}) collective-permute-start(bf16[2,3,168,256]{3,2,1,0:T(8,128)(2,1)S(1)} %pad_maximum_fusion.2.refs_0_.refs_2_), channel_id=1, source_target_pairs={{0,32},{32,64},{64,96},{96,0},{128,160},{160,192},{192,224},{224,1... | collective-permute-start | bytes 1548296 | tf_op jit(solution)/shard_map/ppermute | solution.py:28
  145.1 5.5 %input_part.3 = (f32[256,1024]{1,0:T(8,128)}, bf16[256,1024]{1,0:T(8,128)(2,1)}) custom-call(s32[1]{0:T(128)} %bitcast.y_ref, bf16[4,168,1024]{2,1,0:T(8,128)(2,1)} %bitcast.39, bf16[4,168,1024]{2,1,0:T(8,128)(2,1)} %bitcast.49, bf16[2,3,168,256]{3,2,1,0:T(8,128)(2,1)} %copy-done.13, bf16[2,3,168,256]{3,2,1,0:T(8,128)(2,1)} %copy-done.17, ...), custom_call_target="tpu_custom_call" | custom-call | flops 1409286144 | bytes 6389760 | tf_op jit(solution)/shard_map/input_part/pallas_call | solution.py:55
  150.7 1.4 collective-permute-done.11.refs_3_.refs_5_
  152.1 11.2 %collective-permute-done.10.refs_2_.refs_4_ = bf16[2,3,168,256]{3,2,1,0:T(8,128)(2,1)S(1)} collective-permute-done((bf16[2,3,168,256]{3,2,1,0:T(8,128)(2,1)S(1)}, bf16[2,3,168,256]{3,2,1,0:T(8,128)(2,1)S(1)}, u32[]{:S(2)}, u32[]{:S(2)}) %collective-permute-start.10) | collective-permute-done | bytes 516128 | tf_op jit(solution)/shard_map/ppermute | solution.py:28
  163.3 0.9 collective-permute-done.9.refs_1_.refs_3_
  164.2 0.9 copy-done.20
  165.1 5.5 %input_part.2 = (f32[256,1024]{1,0:T(8,128)}, bf16[256,1024]{1,0:T(8,128)(2,1)}) custom-call(s32[1]{0:T(128)} %bitcast.y_ref, bf16[4,168,1024]{2,1,0:T(8,128)(2,1)} %bitcast.40, bf16[4,168,1024]{2,1,0:T(8,128)(2,1)} %bitcast.50, bf16[2,3,168,256]{3,2,1,0:T(8,128)(2,1)} %copy-done.14, bf16[2,3,168,256]{3,2,1,0:T(8,128)(2,1)} %copy-done.20, ...), custom_call_target="tpu_custom_call" | custom-call | flops 1409286144 | bytes 6389760 | tf_op jit(solution)/shard_map/input_part/pallas_call | solution.py:55
  170.8 2.1 %collective-permute-start.25 = (bf16[128,1024]{1,0:T(8,128)(2,1)S(1)}, bf16[128,1024]{1,0:T(8,128)(2,1)S(1)}, u32[]{:S(2)}, u32[]{:S(2)}) collective-permute-start(bf16[128,1024]{1,0:T(8,128)(2,1)S(1)} %get-tuple-element.38), channel_id=1, source_target_pairs={{0,4},{1,5},{2,6},{3,7},{4,0},{5,1},{6,2},{7,3},{8,12},{9,13},{10,... | collective-permute-start | bytes 786440 | tf_op jit(solution)/shard_map/ppermute | solution.py:43
  172.9 1.5 collective-permute-start.26
  174.7 1.8 collective-permute-start.13
  176.5 5.1 %collective-permute-done.25 = bf16[128,1024]{1,0:T(8,128)(2,1)S(1)} collective-permute-done((bf16[128,1024]{1,0:T(8,128)(2,1)S(1)}, bf16[128,1024]{1,0:T(8,128)(2,1)S(1)}, u32[]{:S(2)}, u32[]{:S(2)}) %collective-permute-start.25) | collective-permute-done | bytes 262176 | tf_op jit(solution)/shard_map/ppermute | solution.py:43
  181.6 5.2 %collective-permute-done.26 = bf16[128,1024]{1,0:T(8,128)(2,1)S(1)} collective-permute-done((bf16[128,1024]{1,0:T(8,128)(2,1)S(1)}, bf16[128,1024]{1,0:T(8,128)(2,1)S(1)}, u32[]{:S(2)}, u32[]{:S(2)}) %collective-permute-start.26) | collective-permute-done | bytes 262176 | tf_op jit(solution)/shard_map/ppermute | solution.py:43
  186.9 3.7 %collective-permute-start.27 = (bf16[32,1024]{1,0:T(8,128)(2,1)S(1)}, bf16[32,1024]{1,0:T(8,128)(2,1)S(1)}, u32[]{:S(2)}, u32[]{:S(2)}) collective-permute-start(bf16[32,1024]{1,0:T(8,128)(2,1)S(1)} %get-tuple-element.40), channel_id=1, source_target_pairs={{0,24},{1,25},{2,26},{3,27},{4,28},{5,29},{6,30},{7,31},{8,0},{9,1... | collective-permute-start | bytes 196616 | tf_op jit(solution)/shard_map/ppermute | solution.py:43
  190.7 2.4 %collective-permute-start.28 = (bf16[32,1024]{1,0:T(8,128)(2,1)S(1)}, bf16[32,1024]{1,0:T(8,128)(2,1)S(1)}, u32[]{:S(2)}, u32[]{:S(2)}) collective-permute-start(bf16[32,1024]{1,0:T(8,128)(2,1)S(1)} %get-tuple-element.42), channel_id=1, source_target_pairs={{0,16},{1,17},{2,18},{3,19},{4,20},{5,21},{6,22},{7,23},{8,24},{9,... | collective-permute-start | bytes 196616 | tf_op jit(solution)/shard_map/ppermute | solution.py:43
  193.1 9.2 %weight_grads.1 = (bf16[4,168,1024]{2,1,0:T(8,128)(2,1)}, bf16[4,168,1024]{2,1,0:T(8,128)(2,1)}, bf16[4,168,1024]{2,1,0:T(8,128)(2,1)}) custom-call(s32[1]{0:T(128)} %bitcast.y_ref, bf16[2,256,1024]{2,1,0:T(8,128)(2,1)} %copy-done, bf16[2,256,1024]{2,1,0:T(8,128)(2,1)} %collective-permute-done.4.refs_1_, bf16[2,3,168,256]{3,2,1,0:T(8,128)(2,1)} %copy-done.14, ...), custom_call_target="tpu_custom_call" | custom-call | flops 4227858432 | bytes 12451840 | tf_op jit(solution)/shard_map/weight_grads/pallas_call | solution.py:55
  (80 shorter events, 8.3 us)
Async XLA Ops:
  1.5 13.7 %collective-permute-start.1 = (bf16[2,32,1024]{2,1,0:T(8,128)(2,1)S(1)}, bf16[2,32,1024]{2,1,0:T(8,128)(2,1)S(1)}, u32[]{:S(2)}, u32[]{:S(2)}) collective-permute-start(bf16[2,32,1024]{2,1,0:T(8,128)(2,1)S(1)} %get-tuple-element.44), channel_id=1, source_target_pairs={{0,16},{1,17},{2,18},{3,19},{4,20},{5,21},{6,22},{7,23},{8,24},{9,... | collective-permute-start | bytes 393224 | tf_op jit(solution)/shard_map/ppermute | solution.py:43
  8.8 10.6 %collective-permute-start = (bf16[2,32,1024]{2,1,0:T(8,128)(2,1)S(1)}, bf16[2,32,1024]{2,1,0:T(8,128)(2,1)S(1)}, u32[]{:S(2)}, u32[]{:S(2)}) collective-permute-start(bf16[2,32,1024]{2,1,0:T(8,128)(2,1)S(1)} %get-tuple-element.44), channel_id=1, source_target_pairs={{0,8},{1,9},{2,10},{3,11},{4,12},{5,13},{6,14},{7,15},{8,16},{9,17... | collective-permute-start | bytes 393224 | tf_op jit(solution)/shard_map/ppermute | solution.py:43
  10.3 11.1 %collective-permute-start.2 = (bf16[2,32,1024]{2,1,0:T(8,128)(2,1)S(1)}, bf16[2,32,1024]{2,1,0:T(8,128)(2,1)S(1)}, u32[]{:S(2)}, u32[]{:S(2)}) collective-permute-start(bf16[2,32,1024]{2,1,0:T(8,128)(2,1)S(1)} %get-tuple-element.44), channel_id=1, source_target_pairs={{0,24},{1,25},{2,26},{3,27},{4,28},{5,29},{6,30},{7,31},{8,0},{9,1... | collective-permute-start | bytes 393224 | tf_op jit(solution)/shard_map/ppermute | solution.py:43
  21.4 16.4 %collective-permute-start.14 = (bf16[2,128,1024]{2,1,0:T(8,128)(2,1)S(1)}, bf16[2,128,1024]{2,1,0:T(8,128)(2,1)S(1)}, u32[]{:S(2)}, u32[]{:S(2)}) collective-permute-start(bf16[2,128,1024]{2,1,0:T(8,128)(2,1)S(1)} %bitcast.51), channel_id=1, source_target_pairs={{0,4},{1,5},{2,6},{3,7},{4,0},{5,1},{6,2},{7,3},{8,12},{9,13},{10,... | collective-permute-start | bytes 1572872 | tf_op jit(solution)/shard_map/ppermute | solution.py:43
  24.6 23.6 %collective-permute-start.15 = (bf16[2,128,1024]{2,1,0:T(8,128)(2,1)S(1)}, bf16[2,128,1024]{2,1,0:T(8,128)(2,1)S(1)}, u32[]{:S(2)}, u32[]{:S(2)}) collective-permute-start(bf16[2,128,1024]{2,1,0:T(8,128)(2,1)S(1)} %bitcast.52), channel_id=1, source_target_pairs={{0,6},{1,7},{2,0},{3,1},{4,2},{5,3},{6,4},{7,5},{8,14},{9,15},{10,... | collective-permute-start | bytes 1572872 | tf_op jit(solution)/shard_map/ppermute | solution.py:43
  25.7 22.6 %collective-permute-start.3 = (bf16[2,128,1024]{2,1,0:T(8,128)(2,1)S(1)}, bf16[2,128,1024]{2,1,0:T(8,128)(2,1)S(1)}, u32[]{:S(2)}, u32[]{:S(2)}) collective-permute-start(bf16[2,128,1024]{2,1,0:T(8,128)(2,1)S(1)} %bitcast.53), channel_id=1, source_target_pairs={{0,2},{1,3},{2,4},{3,5},{4,6},{5,7},{6,0},{7,1},{8,10},{9,11},{10,... | collective-permute-start | bytes 1572872 | tf_op jit(solution)/shard_map/ppermute | solution.py:43
  48.2 2.8 %copy-start.1 = (bf16[2,256,1024]{2,1,0:T(8,128)(2,1)}, bf16[2,256,1024]{2,1,0:T(8,128)(2,1)S(1)}, u32[]{:S(2)}) copy-start(bf16[2,256,1024]{2,1,0:T(8,128)(2,1)S(1)} %constant_dynamic-update-slice_fusion.refs_0_.refs_6_) | copy-start | bytes 3145732
  48.2 2.7 %collective-permute-start.16 = (bf16[2,256,1024]{2,1,0:T(8,128)(2,1)S(1)}, bf16[2,256,1024]{2,1,0:T(8,128)(2,1)S(1)}, u32[]{:S(2)}, u32[]{:S(2)}) collective-permute-start(bf16[2,256,1024]{2,1,0:T(8,128)(2,1)S(1)} %constant_dynamic-update-slice_fusion.refs_0_.refs_6_), channel_id=1, source_target_pairs={{0,1},{1,0},{2,3},{3,2},{4,5},{5,4},{6,7},{7,6},{8,9},{9,8},{10,11... | collective-permute-start | bytes 3145736 | tf_op jit(solution)/shard_map/ppermute | solution.py:43
  48.4 10.0 %copy-start = (bf16[2,256,1024]{2,1,0:T(8,128)(2,1)}, bf16[2,256,1024]{2,1,0:T(8,128)(2,1)S(1)}, u32[]{:S(2)}) copy-start(bf16[2,256,1024]{2,1,0:T(8,128)(2,1)S(1)} %pad_maximum_fusion.refs_0_) | copy-start | bytes 3145732
  48.4 14.3 %collective-permute-start.4 = (bf16[2,256,1024]{2,1,0:T(8,128)(2,1)S(1)}, bf16[2,256,1024]{2,1,0:T(8,128)(2,1)}, u32[]{:S(2)}, u32[]{:S(2)}) collective-permute-start(bf16[2,256,1024]{2,1,0:T(8,128)(2,1)S(1)} %pad_maximum_fusion.refs_0_), channel_id=1, source_target_pairs={{0,1},{1,0},{2,3},{3,2},{4,5},{5,4},{6,7},{7,6},{8,9},{9,8},{10,11... | collective-permute-start | bytes 3145736 | tf_op jit(solution)/shard_map/ppermute | solution.py:43
  51.0 1.0 copy-start.2
  58.4 16.4 %collective-permute-start.17 = (bf16[2,3,168,256]{3,2,1,0:T(8,128)(2,1)}, bf16[2,3,168,256]{3,2,1,0:T(8,128)(2,1)S(1)}, u32[]{:S(2)}, u32[]{:S(2)}) collective-permute-start(bf16[2,3,168,256]{3,2,1,0:T(8,128)(2,1)} %get-tuple-element.22), channel_id=1, source_target_pairs={{0,64},{32,96},{64,0},{96,32},{128,192},{160,224},{192,128},{224,1... | collective-permute-start | bytes 1548296 | tf_op jit(solution)/shard_map/ppermute | solution.py:28
  60.7 25.2 %collective-permute-start.18 = (bf16[2,3,168,256]{3,2,1,0:T(8,128)(2,1)}, bf16[2,3,168,256]{3,2,1,0:T(8,128)(2,1)S(1)}, u32[]{:S(2)}, u32[]{:S(2)}) collective-permute-start(bf16[2,3,168,256]{3,2,1,0:T(8,128)(2,1)} %get-tuple-element.23), channel_id=1, source_target_pairs={{0,32},{32,64},{64,96},{96,0},{128,160},{160,192},{192,224},{224,1... | collective-permute-start | bytes 1548296 | tf_op jit(solution)/shard_map/ppermute | solution.py:28
  60.7 25.2 %collective-permute-start.19 = (bf16[2,3,168,256]{3,2,1,0:T(8,128)(2,1)}, bf16[2,3,168,256]{3,2,1,0:T(8,128)(2,1)S(1)}, u32[]{:S(2)}, u32[]{:S(2)}) collective-permute-start(bf16[2,3,168,256]{3,2,1,0:T(8,128)(2,1)} %get-tuple-element.24), channel_id=1, source_target_pairs={{0,96},{32,0},{64,32},{96,64},{128,224},{160,128},{192,160},{224,1... | collective-permute-start | bytes 1548296 | tf_op jit(solution)/shard_map/ppermute | solution.py:28
  69.2 27.7 %collective-permute-start.5 = (bf16[2,3,168,256]{3,2,1,0:T(8,128)(2,1)}, bf16[2,3,168,256]{3,2,1,0:T(8,128)(2,1)S(1)}, u32[]{:S(2)}, u32[]{:S(2)}) collective-permute-start(bf16[2,3,168,256]{3,2,1,0:T(8,128)(2,1)} %get-tuple-element.17), channel_id=1, source_target_pairs={{0,64},{32,96},{64,0},{96,32},{128,192},{160,224},{192,128},{224,1... | collective-permute-start | bytes 1548296 | tf_op jit(solution)/shard_map/ppermute | solution.py:28
  70.6 36.7 %collective-permute-start.6 = (bf16[2,3,168,256]{3,2,1,0:T(8,128)(2,1)}, bf16[2,3,168,256]{3,2,1,0:T(8,128)(2,1)S(1)}, u32[]{:S(2)}, u32[]{:S(2)}) collective-permute-start(bf16[2,3,168,256]{3,2,1,0:T(8,128)(2,1)} %get-tuple-element.18), channel_id=1, source_target_pairs={{0,32},{32,64},{64,96},{96,0},{128,160},{160,192},{192,224},{224,1... | collective-permute-start | bytes 1548296 | tf_op jit(solution)/shard_map/ppermute | solution.py:28
  74.8 11.2 %copy-start.7 = (bf16[2,3,168,256]{3,2,1,0:T(8,128)(2,1)}, bf16[2,3,168,256]{3,2,1,0:T(8,128)(2,1)S(1)}, u32[]{:S(2)}) copy-start(bf16[2,3,168,256]{3,2,1,0:T(8,128)(2,1)S(1)} %collective-permute-done.17.refs_5_) | copy-start | bytes 1548292
  74.8 32.5 %collective-permute-start.7 = (bf16[2,3,168,256]{3,2,1,0:T(8,128)(2,1)}, bf16[2,3,168,256]{3,2,1,0:T(8,128)(2,1)S(1)}, u32[]{:S(2)}, u32[]{:S(2)}) collective-permute-start(bf16[2,3,168,256]{3,2,1,0:T(8,128)(2,1)} %get-tuple-element.19), channel_id=1, source_target_pairs={{0,96},{32,0},{64,32},{96,64},{128,224},{160,128},{192,160},{224,1... | collective-permute-start | bytes 1548296 | tf_op jit(solution)/shard_map/ppermute | solution.py:28
  92.0 24.1 %copy-start.4 = (f32[2,3,168,256]{3,2,1,0:T(8,128)S(1)}, f32[2,3,168,256]{3,2,1,0:T(8,128)}, u32[]{:S(2)}) copy-start(f32[2,3,168,256]{3,2,1,0:T(8,128)} %partial_own.3) | copy-start | bytes 3096580
  92.0 24.1 %collective-permute-start.20 = (f32[2,3,168,256]{3,2,1,0:T(8,128)}, f32[2,3,168,256]{3,2,1,0:T(8,128)S(1)}, u32[]{:S(2)}, u32[]{:S(2)}) collective-permute-start(f32[2,3,168,256]{3,2,1,0:T(8,128)} %partial_own.3), channel_id=1, source_target_pairs={{0,128},{32,160},{64,192},{96,224},{128,0},{160,32},{192,64},{224,... | collective-permute-start | bytes 3096584 | tf_op jit(solution)/shard_map/ppermute | solution.py:32
  96.9 10.4 %copy-start.8 = (bf16[2,3,168,256]{3,2,1,0:T(8,128)(2,1)}, bf16[2,3,168,256]{3,2,1,0:T(8,128)(2,1)S(1)}, u32[]{:S(2)}) copy-start(bf16[2,3,168,256]{3,2,1,0:T(8,128)(2,1)S(1)} %collective-permute-done.5.refs_5_) | copy-start | bytes 1548292
  108.1 0.8 copy-start.12
  113.4 24.6 %collective-permute-start.8 = (f32[2,3,168,256]{3,2,1,0:T(8,128)}, f32[2,3,168,256]{3,2,1,0:T(8,128)S(1)}, u32[]{:S(2)}, u32[]{:S(2)}) collective-permute-start(f32[2,3,168,256]{3,2,1,0:T(8,128)} %partial_own.2), channel_id=1, source_target_pairs={{0,128},{32,160},{64,192},{96,224},{128,0},{160,32},{192,64},{224,... | collective-permute-start | bytes 3096584 | tf_op jit(solution)/shard_map/ppermute | solution.py:32
  116.3 21.7 %copy-start.3 = (f32[2,3,168,256]{3,2,1,0:T(8,128)S(1)}, f32[2,3,168,256]{3,2,1,0:T(8,128)}, u32[]{:S(2)}) copy-start(f32[2,3,168,256]{3,2,1,0:T(8,128)} %partial_own.2) | copy-start | bytes 3096580
  116.6 21.6 %copy-start.13 = (bf16[2,3,168,256]{3,2,1,0:T(8,128)(2,1)}, bf16[2,3,168,256]{3,2,1,0:T(8,128)(2,1)S(1)}, u32[]{:S(2)}) copy-start(bf16[2,3,168,256]{3,2,1,0:T(8,128)(2,1)S(1)} %pad_maximum_fusion.3.refs_0_.refs_8_) | copy-start | bytes 1548292
  116.6 24.3 %collective-permute-start.23 = (bf16[2,3,168,256]{3,2,1,0:T(8,128)(2,1)S(1)}, bf16[2,3,168,256]{3,2,1,0:T(8,128)(2,1)S(1)}, u32[]{:S(2)}, u32[]{:S(2)}) collective-permute-start(bf16[2,3,168,256]{3,2,1,0:T(8,128)(2,1)S(1)} %pad_maximum_fusion.3.refs_0_.refs_8_), channel_id=1, source_target_pairs={{0,96},{32,0},{64,32},{96,64},{128,224},{160,128},{192,160},{224,1... | collective-permute-start | bytes 1548296 | tf_op jit(solution)/shard_map/ppermute | solution.py:28
  118.2 25.3 %collective-permute-start.22 = (bf16[2,3,168,256]{3,2,1,0:T(8,128)(2,1)S(1)}, bf16[2,3,168,256]{3,2,1,0:T(8,128)(2,1)S(1)}, u32[]{:S(2)}, u32[]{:S(2)}) collective-permute-start(bf16[2,3,168,256]{3,2,1,0:T(8,128)(2,1)S(1)} %pad_maximum_fusion.3.refs_0_.refs_8_), channel_id=1, source_target_pairs={{0,64},{32,96},{64,0},{96,32},{128,192},{160,224},{192,128},{224,1... | collective-permute-start | bytes 1548296 | tf_op jit(solution)/shard_map/ppermute | solution.py:28
  119.3 24.1 %collective-permute-start.21 = (bf16[2,3,168,256]{3,2,1,0:T(8,128)(2,1)S(1)}, bf16[2,3,168,256]{3,2,1,0:T(8,128)(2,1)S(1)}, u32[]{:S(2)}, u32[]{:S(2)}) collective-permute-start(bf16[2,3,168,256]{3,2,1,0:T(8,128)(2,1)S(1)} %pad_maximum_fusion.3.refs_0_.refs_8_), channel_id=1, source_target_pairs={{0,32},{32,64},{64,96},{96,0},{128,160},{160,192},{192,224},{224,1... | collective-permute-start | bytes 1548296 | tf_op jit(solution)/shard_map/ppermute | solution.py:28
  138.4 12.1 %copy-start.14 = (bf16[2,3,168,256]{3,2,1,0:T(8,128)(2,1)}, bf16[2,3,168,256]{3,2,1,0:T(8,128)(2,1)S(1)}, u32[]{:S(2)}) copy-start(bf16[2,3,168,256]{3,2,1,0:T(8,128)(2,1)S(1)} %pad_maximum_fusion.2.refs_0_.refs_2_) | copy-start | bytes 1548292
  138.4 13.6 %collective-permute-start.11 = (bf16[2,3,168,256]{3,2,1,0:T(8,128)(2,1)S(1)}, bf16[2,3,168,256]{3,2,1,0:T(8,128)(2,1)S(1)}, u32[]{:S(2)}, u32[]{:S(2)}) collective-permute-start(bf16[2,3,168,256]{3,2,1,0:T(8,128)(2,1)S(1)} %pad_maximum_fusion.2.refs_0_.refs_2_), channel_id=1, source_target_pairs={{0,96},{32,0},{64,32},{96,64},{128,224},{160,128},{192,160},{224,1... | collective-permute-start | bytes 1548296 | tf_op jit(solution)/shard_map/ppermute | solution.py:28
  139.7 23.6 %collective-permute-start.10 = (bf16[2,3,168,256]{3,2,1,0:T(8,128)(2,1)S(1)}, bf16[2,3,168,256]{3,2,1,0:T(8,128)(2,1)S(1)}, u32[]{:S(2)}, u32[]{:S(2)}) collective-permute-start(bf16[2,3,168,256]{3,2,1,0:T(8,128)(2,1)S(1)} %pad_maximum_fusion.2.refs_0_.refs_2_), channel_id=1, source_target_pairs={{0,64},{32,96},{64,0},{96,32},{128,192},{160,224},{192,128},{224,1... | collective-permute-start | bytes 1548296 | tf_op jit(solution)/shard_map/ppermute | solution.py:28
  140.9 2.5 %copy-start.15 = (bf16[2,3,168,256]{3,2,1,0:T(8,128)(2,1)}, bf16[2,3,168,256]{3,2,1,0:T(8,128)(2,1)S(1)}, u32[]{:S(2)}) copy-start(bf16[2,3,168,256]{3,2,1,0:T(8,128)(2,1)S(1)} %collective-permute-done.23.refs_3_.refs_11_) | copy-start | bytes 1548292
  140.9 23.3 %collective-permute-start.9 = (bf16[2,3,168,256]{3,2,1,0:T(8,128)(2,1)S(1)}, bf16[2,3,168,256]{3,2,1,0:T(8,128)(2,1)S(1)}, u32[]{:S(2)}, u32[]{:S(2)}) collective-permute-start(bf16[2,3,168,256]{3,2,1,0:T(8,128)(2,1)S(1)} %pad_maximum_fusion.2.refs_0_.refs_2_), channel_id=1, source_target_pairs={{0,32},{32,64},{64,96},{96,0},{128,160},{160,192},{192,224},{224,1... | collective-permute-start | bytes 1548296 | tf_op jit(solution)/shard_map/ppermute | solution.py:28
  143.4 0.8 copy-start.16
  144.2 0.8 copy-start.17
  150.6 20.1 %copy-start.6 = (f32[256,1024]{1,0:T(8,128)S(1)}, f32[256,1024]{1,0:T(8,128)}, u32[]{:S(2)}) copy-start(f32[256,1024]{1,0:T(8,128)} %get-tuple-element.25) | copy-start | bytes 3145732
  150.6 20.1 %collective-permute-start.24 = (bf16[256,1024]{1,0:T(8,128)(2,1)}, bf16[256,1024]{1,0:T(8,128)(2,1)S(1)}, u32[]{:S(2)}, u32[]{:S(2)}) collective-permute-start(bf16[256,1024]{1,0:T(8,128)(2,1)} %get-tuple-element.26), channel_id=1, source_target_pairs={{0,1},{1,0},{2,3},{3,2},{4,5},{5,4},{6,7},{7,6},{8,9},{9,8},{10,11... | collective-permute-start | bytes 1572872 | tf_op jit(solution)/shard_map/ppermute | solution.py:43
  152.1 12.2 %copy-start.18 = (bf16[2,3,168,256]{3,2,1,0:T(8,128)(2,1)}, bf16[2,3,168,256]{3,2,1,0:T(8,128)(2,1)S(1)}, u32[]{:S(2)}) copy-start(bf16[2,3,168,256]{3,2,1,0:T(8,128)(2,1)S(1)} %collective-permute-done.11.refs_3_.refs_5_) | copy-start | bytes 1548292
  163.3 0.9 copy-start.19
  164.2 0.9 copy-start.20
  170.6 3.8 %collective-permute-start.12 = (bf16[256,1024]{1,0:T(8,128)(2,1)}, bf16[256,1024]{1,0:T(8,128)(2,1)S(1)}, u32[]{:S(2)}, u32[]{:S(2)}) collective-permute-start(bf16[256,1024]{1,0:T(8,128)(2,1)} %get-tuple-element.21), channel_id=1, source_target_pairs={{0,1},{1,0},{2,3},{3,2},{4,5},{5,4},{6,7},{7,6},{8,9},{9,8},{10,11... | collective-permute-start | bytes 1572872 | tf_op jit(solution)/shard_map/ppermute | solution.py:43
  170.6 3.8 %copy-start.5 = (f32[256,1024]{1,0:T(8,128)S(1)}, f32[256,1024]{1,0:T(8,128)}, u32[]{:S(2)}) copy-start(f32[256,1024]{1,0:T(8,128)} %get-tuple-element.20) | copy-start | bytes 3145732
  170.8 10.7 %collective-permute-start.25 = (bf16[128,1024]{1,0:T(8,128)(2,1)S(1)}, bf16[128,1024]{1,0:T(8,128)(2,1)S(1)}, u32[]{:S(2)}, u32[]{:S(2)}) collective-permute-start(bf16[128,1024]{1,0:T(8,128)(2,1)S(1)} %get-tuple-element.38), channel_id=1, source_target_pairs={{0,4},{1,5},{2,6},{3,7},{4,0},{5,1},{6,2},{7,3},{8,12},{9,13},{10,... | collective-permute-start | bytes 786440 | tf_op jit(solution)/shard_map/ppermute | solution.py:43
  172.9 13.8 %collective-permute-start.26 = (bf16[128,1024]{1,0:T(8,128)(2,1)S(1)}, bf16[128,1024]{1,0:T(8,128)(2,1)S(1)}, u32[]{:S(2)}, u32[]{:S(2)}) collective-permute-start(bf16[128,1024]{1,0:T(8,128)(2,1)S(1)} %get-tuple-element.39), channel_id=1, source_target_pairs={{0,2},{1,3},{2,4},{3,5},{4,6},{5,7},{6,0},{7,1},{8,10},{9,11},{10,... | collective-permute-start | bytes 786440 | tf_op jit(solution)/shard_map/ppermute | solution.py:43
  174.7 12.1 %collective-permute-start.13 = (bf16[128,1024]{1,0:T(8,128)(2,1)S(1)}, bf16[128,1024]{1,0:T(8,128)(2,1)S(1)}, u32[]{:S(2)}, u32[]{:S(2)}) collective-permute-start(bf16[128,1024]{1,0:T(8,128)(2,1)S(1)} %slice.111), channel_id=1, source_target_pairs={{0,6},{1,7},{2,0},{3,1},{4,2},{5,3},{6,4},{7,5},{8,14},{9,15},{10,... | collective-permute-start | bytes 786440 | tf_op jit(solution)/shard_map/ppermute | solution.py:43
  186.9 15.4 %collective-permute-start.27 = (bf16[32,1024]{1,0:T(8,128)(2,1)S(1)}, bf16[32,1024]{1,0:T(8,128)(2,1)S(1)}, u32[]{:S(2)}, u32[]{:S(2)}) collective-permute-start(bf16[32,1024]{1,0:T(8,128)(2,1)S(1)} %get-tuple-element.40), channel_id=1, source_target_pairs={{0,24},{1,25},{2,26},{3,27},{4,28},{5,29},{6,30},{7,31},{8,0},{9,1... | collective-permute-start | bytes 196616 | tf_op jit(solution)/shard_map/ppermute | solution.py:43
  190.7 11.7 %collective-permute-start.29 = (bf16[32,1024]{1,0:T(8,128)(2,1)S(1)}, bf16[32,1024]{1,0:T(8,128)(2,1)S(1)}, u32[]{:S(2)}, u32[]{:S(2)}) collective-permute-start(bf16[32,1024]{1,0:T(8,128)(2,1)S(1)} %get-tuple-element.41), channel_id=1, source_target_pairs={{0,8},{1,9},{2,10},{3,11},{4,12},{5,13},{6,14},{7,15},{8,16},{9,17... | collective-permute-start | bytes 196616 | tf_op jit(solution)/shard_map/ppermute | solution.py:43
  190.7 11.7 %collective-permute-start.28 = (bf16[32,1024]{1,0:T(8,128)(2,1)S(1)}, bf16[32,1024]{1,0:T(8,128)(2,1)S(1)}, u32[]{:S(2)}, u32[]{:S(2)}) collective-permute-start(bf16[32,1024]{1,0:T(8,128)(2,1)S(1)} %get-tuple-element.42), channel_id=1, source_target_pairs={{0,16},{1,17},{2,18},{3,19},{4,20},{5,21},{6,22},{7,23},{8,24},{9,... | collective-permute-start | bytes 196616 | tf_op jit(solution)/shard_map/ppermute | solution.py:43
  (3 other events, 2.4 us)
